TPU v7x, 512 devices: a whole 4x8x8 slice. The times are simulated.
512 devices in a mesh: seq: 16 (over y, core), wide: 32 (over z, x).
Axes of the slice: x: 4, y: 8, z: 8, core: 2. Of those that a mesh axis runs over, the one named last changes fastest.
Arguments:
- out_gate: bfloat16 [65536, 4096], P(('seq', 'wide')), may hold values from -6 to 6
- in_gate: bfloat16 [65536, 4096], P(('seq', 'wide')), may hold values from -6 to 6
- values: bfloat16 [65536, 4096], P(('seq', 'wide')), may hold values from -6 to 6
- filter_taps: bfloat16 [4096, 4096], P('seq', 'wide'), may hold values from -0.09375 to 0.09375
- skip_gain: float32 [4096], P('wide'), may hold values from 0.5 to 1.5
Outputs:
- mixed: bfloat16 [65536, 4096], P(('seq', 'wide'))
All inputs are finite; a program needn't handle non-finite values.
Results may differ from a plain program's by a relative error of at most 0.0065.
Values may be sent and summed in bfloat16 or wider, within the bound.
A program may use at most 64 MiB of HBM per device.

v0:
```python
import math
import jax
import jax.numpy as jnp
from jax import lax
from jax.sharding import PartitionSpec as P

PRECISE = lax.Precision.HIGH


def passed_along(value, axis, by):
    length = lax.axis_size(axis)
    pairs = [(i, i + by) for i in range(length) if 0 <= i + by < length]
    return lax.ppermute(value, axis, pairs)


def phase_table(first_count, second_count, modulus):
    first_index = lax.iota(jnp.int32, first_count)
    second_index = lax.iota(jnp.int32, second_count)
    product = first_index[:, None] * second_index[None, :] % modulus
    angle_table = product.astype(jnp.float32) * (-2.0 * math.pi / modulus)
    return (jnp.cos(angle_table), jnp.sin(angle_table))


def column_block(column_count, orientation):
    cosine_table, sine_table = phase_table(column_count, column_count, column_count)
    upper_rows = jnp.stack([cosine_table, orientation * sine_table], axis=1)
    bottom = jnp.stack([-orientation * sine_table, cosine_table], axis=1)
    return jnp.stack([upper_rows, bottom], axis=0)


def rotate(pair_parts, row_count, column_count, padded_size, orientation):
    twist_cosine, twist_sine = phase_table(row_count, column_count, padded_size)
    twist_sine = orientation * twist_sine
    real_part = pair_parts[0] * twist_cosine[:, :, None] - pair_parts[1] * twist_sine[:, :, None]
    imaginary = pair_parts[0] * twist_sine[:, :, None] + pair_parts[1] * twist_cosine[:, :, None]
    return jnp.stack([real_part, imaginary], axis=0)


def causal_filter(signal, tap_columns, padded_size):
    column_count = 64
    channels = signal.shape[1]
    rows_used = max(signal.shape[0], tap_columns.shape[0]) // column_count
    row_count = padded_size // column_count
    half_rows = row_count // 2 + 1
    cosine_first, sine_first = phase_table(row_count, rows_used, row_count)
    first_table = jnp.concatenate(
        [
            jnp.concatenate([cosine_first, -sine_first], axis=1),
            jnp.concatenate([sine_first, cosine_first], axis=1),
        ],
        axis=0,
    )
    joined = jnp.concatenate(
        [
            signal.reshape(rows_used, column_count * channels),
            tap_columns.reshape(rows_used, column_count * channels),
        ],
        axis=0,
    )
    first = jnp.dot(first_table, joined, precision=PRECISE).reshape(
        2, row_count, column_count, channels
    )
    turned = rotate(first, row_count, column_count, padded_size, 1.0)
    spectrum = jnp.einsum(
        "panc,pnqk->qakc", turned, column_block(column_count, 1.0), precision=PRECISE
    )
    kept = spectrum[:, :half_rows]
    zero_row = jnp.roll(jnp.flip(spectrum[:, :1], axis=2), 1, axis=2)
    mirrored = jnp.flip(spectrum[:, row_count // 2 :], axis=(1, 2))
    partner = jnp.concatenate([zero_row, mirrored], axis=1)
    signal_real = 0.5 * (kept[0] + partner[0])
    signal_imag = 0.5 * (kept[1] - partner[1])
    taps_real = 0.5 * (kept[1] + partner[1])
    taps_imag = 0.5 * (partner[0] - kept[0])
    product_real = signal_real * taps_real - signal_imag * taps_imag
    product_imag = signal_real * taps_imag + signal_imag * taps_real
    product = jnp.stack([product_real, product_imag], axis=0)
    mixed = jnp.einsum(
        "pakc,pkqn->qanc", product, column_block(column_count, -1.0), precision=PRECISE
    )
    returned = rotate(mixed, half_rows, column_count, padded_size, -1.0)
    cosine_last, sine_last = phase_table(row_count, half_rows, row_count)
    frequency = lax.iota(jnp.int32, half_rows)
    weights = jnp.where((frequency == 0) | (frequency == row_count // 2), 1.0, 2.0).astype(
        jnp.float32
    )
    last_table = (
        jnp.concatenate([cosine_last * weights[None, :], sine_last * weights[None, :]], axis=1)
        / padded_size
    )
    flattened = returned.reshape(2 * half_rows, column_count * channels)
    result = jnp.dot(last_table, flattened, precision=PRECISE)
    return result.reshape(padded_size, channels)


def local(out_gate, in_gate, values, filter_taps, skip_gain):
    gated_values = (in_gate.astype(jnp.float32) * values.astype(jnp.float32)).astype(jnp.bfloat16)
    all_taps = lax.all_gather(filter_taps, "seq", axis=0, tiled=True)
    by_channel = lax.all_to_all(gated_values, "wide", split_axis=1, concat_axis=0, tiled=True)
    group_length = by_channel.shape[0]
    tap_count = all_taps.shape[0]
    linear = causal_filter(by_channel, all_taps, group_length + tap_count)
    own_part = linear[:group_length]
    future = linear[group_length:]
    incoming = passed_along(future.astype(jnp.bfloat16), "seq", 1).astype(future.dtype)
    convolved = own_part + incoming
    filtered = (convolved + skip_gain[None, :] * by_channel.astype(jnp.float32)).astype(
        jnp.bfloat16
    )
    returned = lax.all_to_all(filtered, "wide", split_axis=0, concat_axis=1, tiled=True)
    return (out_gate.astype(jnp.float32) * returned.astype(jnp.float32)).astype(jnp.bfloat16)


def solution(mesh):
    in_specs = (
        P(("seq", "wide"), None),
        P(("seq", "wide"), None),
        P(("seq", "wide"), None),
        P("seq", "wide"),
        P("wide"),
    )
    out_specs = P(("seq", "wide"), None)
    return jax.shard_map(local, mesh=mesh, in_specs=in_specs, out_specs=out_specs, check_vma=False)
```

profile of v0, /device:TPU:18, one launch (start us, length us, event | category | flops | bytes accessed | tf_op | source)
XLA Modules:
  0.0 184.0 jit_solution(17083957285483094685)
XLA Ops:
  6.5 1.6 copy.25
  8.2 1.6 copy.26
  11.4 13.5 %all-to-all-start = ((bf16[128,32,128]{2,0,1:T(8,128)(2,1)}), bf16[128,32,128]{2,0,1:T(8,128)(2,1)S(1)}, u32[]{:S(2)}, u32[]{:S(2)}) async-start(bf16[128,32,128]{2,0,1:T(8,128)(2,1)} %copy.27), calls=%async_computation | async-start | bytes 2097152 | tf_op jit(solution)/shard_map/all_to_all | solution.py:99
  29.1 39.1 %all-gather.2.cloned.1.call-done = bf16[4096,128]{1,0:T(8,128)(2,1)} async-done(((bf16[256,128]{1,0:T(8,128)(2,1)}), bf16[4096,128]{1,0:T(8,128)(2,1)}) %all-gather.2.cloned.1.call-update) | async-done | bytes 1048592 | tf_op jit(solution)/shard_map/all_gather | solution.py:98
  70.2 3.4 %fusion.16 = f32[256,8192]{1,0:T(8,128)S(1)} fusion(bf16[64,8192]{1,0:T(8,128)(2,1)S(1)} %reshape.233, bf16[64,8192]{1,0:T(8,128)(2,1)S(1)} %reshape.232, f32[128,64]{1,0:T(8,128)} %get-tuple-element.22, f32[128,64]{1,0:T(8,128)S(1)} %get-tuple-element.21, f32[128,64]{1,0:T(8,128)S(1)} %fusion.74), kind=kOutput, calls=%fused_computation.31 | convolution fusion | flops 1614905344 | bytes 10584064 | tf_op jit(solution)/shard_map/dot_general | solution.py:60
  76.0 2.5 %fusion.8 = (f32[1,128,64,128]{3,2,0,1:T(8,128)S(1)}, f32[1,128,64,128]{3,2,0,1:T(8,128)S(1)}) fusion(f32[128,64]{1,0:T(8,128)S(1)} %get-tuple-element.23, f32[128,64]{1,0:T(8,128)S(1)} %get-tuple-element.24, f32[1,128,64,128]{3,2,1,0:T(8,128)S(1)} %bitcast.110, f32[1,128,64,128]{3,2,1,0:T(8,128)S(1)} %bitcast.111), kind=kLoop, calls=%fused_computation.13 | loop fusion | flops 6291456 | bytes 16842752 | tf_op jit(solution)/shard_map/sub | solution.py:34
  78.5 4.3 %fusion.12 = f32[2,128,64,128]{3,2,1,0:T(8,128)S(1)} fusion(f32[1,128,64,128]{3,2,0,1:T(8,128)S(1)} %get-tuple-element.8, f32[1,128,64,128]{3,2,0,1:T(8,128)S(1)} %get-tuple-element.7, f32[1,64,2,64]{1,3,0,2:T(8,128)S(1)} %copy-done.6, f32[1,64,2,64]{1,3,0,2:T(8,128)S(1)} %copy-done.7), kind=kOutput, calls=%fused_computation.20 | convolution fusion | flops 1612726272 | bytes 16842752 | tf_op jit(solution)/shard_map/panc,pnqk->qakc/dot_general | solution.py:64
  82.9 2.8 %slice.86 = f32[2,64,64,128]{3,2,1,0:T(8,128)} slice(f32[2,128,64,128]{3,2,1,0:T(8,128)S(1)} %fusion.12), slice={[0:2], [64:128], [0:64], [0:128]} | slice | bytes 8388608 | tf_op jit(solution)/shard_map/slice | solution.py:69
  85.7 1.7 copy-done
  87.4 6.6 %rev.6 = f32[2,64,64,128]{3,2,1,0:T(8,128)} reverse(f32[2,64,64,128]{3,2,1,0:T(8,128)} %slice.86), dimensions={1,2} | reverse | bytes 8388608 | tf_op jit(solution)/shard_map/jit(_flip)/rev | solution.py:69
  94.0 2.9 %pad_maximum_fusion = f32[2,65,64,128]{3,2,1,0:T(8,128)S(1)} fusion(f32[2,64,64,128]{3,2,1,0:T(8,128)} %rev.6, f32[2,1,63,128]{3,2,1,0:T(8,128)S(1)} %slice.71, f32[2,1,1,128]{3,2,1,0:T(1,128)S(1)} %slice.84), kind=kLoop, calls=%fused_computation.4 | loop fusion | flops 2129920 | bytes 8519680 | tf_op jit(solution)/shard_map/concatenate | solution.py:70
  96.9 1.7 copy-done.1
  98.7 1.5 multiply_subtract_fusion.1
  100.3 2.2 %fusion.13 = f32[2,65,64,128]{3,2,1,0:T(8,128)S(1)} fusion(f32[1,65,64,128]{3,2,1,0:T(8,128)S(1)} %get-tuple-element.6, f32[1,65,64,128]{3,2,1,0:T(8,128)S(1)} %get-tuple-element.5, f32[1,64,2,64]{1,3,2,0:T(8,128)S(1)} %copy-done.5, f32[1,64,2,64]{1,3,2,0:T(8,128)S(1)} %copy-done.4), kind=kOutput, calls=%fused_computation.21 | convolution fusion | flops 818970624 | bytes 8585216 | tf_op jit(solution)/shard_map/pakc,pkqn->qanc/dot_general | solution.py:78
  104.9 3.6 %copy.44 = f32[17,8,64,128]{3,1,2,0:T(8,128)S(1)} copy(f32[17,8,64,128]{3,2,1,0:T(8,128)S(1)} %bitcast.108) | data formatting | bytes 8912896
  108.4 2.1 %fusion.23 = f32[128,8192]{1,0:T(8,128)S(1)} fusion(f32[130,8192]{1,0:T(8,128)S(1)} %bitcast.107, f32[128,65]{1,0:T(8,128)S(1)} %get-tuple-element.20, f32[128,65]{1,0:T(8,128)S(1)} %get-tuple-element.19), kind=kOutput, calls=%fused_computation.42 | convolution fusion | flops 817922560 | bytes 8520704 | tf_op jit(solution)/shard_map/dot_general | solution.py:92
  110.6 1.9 %copy-done.2 = f32[128,8192]{1,0:T(8,128)} copy-done((f32[128,8192]{1,0:T(8,128)}, f32[128,8192]{1,0:T(8,128)S(1)}, u32[]{:S(2)}) %copy-start.2) | copy-done | bytes 4194328
  113.6 2.5 %convert_element_type.128 = bf16[4096,128]{1,0:T(8,128)(2,1)} reshape(bf16[64,8192]{1,0:T(8,128)(2,1)} %slice.141) | data formatting | bytes 2097152 | tf_op jit(solution)/shard_map/convert_element_type | solution.py:105
  116.1 2.3 %collective-permute-start = (bf16[4096,128]{1,0:T(8,128)(2,1)}, bf16[4096,128]{1,0:T(8,128)(2,1)}, u32[]{:S(2)}, u32[]{:S(2)}) collective-permute-start(bf16[4096,128]{1,0:T(8,128)(2,1)} %convert_element_type.128), channel_id=1, source_target_pairs={{0,32},{32,64},{64,96},{96,128},{128,160},{160,192},{192,224},{224... | collective-permute-start | bytes 3145736 | tf_op jit(solution)/shard_map/ppermute | solution.py:13
  118.4 1.5 slice.79
  119.9 12.7 %collective-permute-done = bf16[4096,128]{1,0:T(8,128)(2,1)} collective-permute-done((bf16[4096,128]{1,0:T(8,128)(2,1)}, bf16[4096,128]{1,0:T(8,128)(2,1)}, u32[]{:S(2)}, u32[]{:S(2)}) %collective-permute-start) | collective-permute-done | bytes 1048608 | tf_op jit(solution)/shard_map/ppermute | solution.py:13
  132.7 3.2 %fusion.22 = bf16[4096,128]{1,0:T(8,128)(2,1)} fusion(f32[4096,128]{1,0:T(8,128)} %slice.79, bf16[4096,128]{1,0:T(8,128)(2,1)} %collective-permute-done, bf16[128,32,128]{2,0,1:T(8,128)(2,1)S(1)} %all-to-all-done, f32[128]{0:T(128)S(1)} %copy-done.10), kind=kLoop, calls=%fused_computation.39 | loop fusion | flops 3145728 | bytes 5243392 | tf_op jit(solution)/shard_map/convert_element_type | solution.py:107
  135.9 10.6 %all-to-all-start.1 = ((bf16[32,128,128]{2,1,0:T(8,128)(2,1)}), bf16[32,128,128]{2,1,0:T(8,128)(2,1)S(1)}, u32[]{:S(2)}, u32[]{:S(2)}) async-start(bf16[32,128,128]{2,1,0:T(8,128)(2,1)} %bitcast.25), calls=%async_computation.1 | async-start | bytes 2097152 | tf_op jit(solution)/shard_map/all_to_all | solution.py:110
  147.2 27.7 %all-to-all-done.1 = bf16[32,128,128]{2,1,0:T(8,128)(2,1)S(1)} async-done(((bf16[32,128,128]{2,1,0:T(8,128)(2,1)}), bf16[32,128,128]{2,1,0:T(8,128)(2,1)S(1)}, u32[]{:S(2)}, u32[]{:S(2)}) %all-to-all-start.1) | async-done | bytes 1048608 | tf_op jit(solution)/shard_map/all_to_all | solution.py:110
  (51 shorter events, 16.6 us)
Async XLA Ops:
  11.4 58.4 %all-to-all-start = ((bf16[128,32,128]{2,0,1:T(8,128)(2,1)}), bf16[128,32,128]{2,0,1:T(8,128)(2,1)S(1)}, u32[]{:S(2)}, u32[]{:S(2)}) async-start(bf16[128,32,128]{2,0,1:T(8,128)(2,1)} %copy.27), calls=%async_computation | async-start | bytes 2097152 | tf_op jit(solution)/shard_map/all_to_all | solution.py:99
  24.8 43.4 %all-gather.2.cloned.1.call-start = ((), (), s32[]{:S(2)}) async-start(), calls=%async_computation.2 | async-start | bytes 1114112 | tf_op jit(solution)/shard_map/all_gather | solution.py:98
  76.0 2.5 %copy-start.6 = (f32[1,64,2,64]{1,3,0,2:T(8,128)S(1)}, f32[1,64,2,64]{1,3,0,2:T(8,128)}, u32[]{:S(2)}) copy-start(f32[1,64,2,64]{1,3,0,2:T(8,128)} %get-tuple-element.14) | copy-start | bytes 98308
  76.0 2.5 %copy-start.7 = (f32[1,64,2,64]{1,3,0,2:T(8,128)S(1)}, f32[1,64,2,64]{1,3,0,2:T(8,128)}, u32[]{:S(2)}) copy-start(f32[1,64,2,64]{1,3,0,2:T(8,128)} %get-tuple-element.17) | copy-start | bytes 98308
  82.9 4.5 %copy-start = (f32[2,128,64,128]{3,2,1,0:T(8,128)}, f32[2,128,64,128]{3,2,1,0:T(8,128)S(1)}, u32[]{:S(2)}) copy-start(f32[2,128,64,128]{3,2,1,0:T(8,128)S(1)} %fusion.12) | copy-start | bytes 25165828
  94.0 4.6 %copy-start.1 = (f32[2,128,64,128]{3,2,1,0:T(8,128)S(1)}, f32[2,128,64,128]{3,2,1,0:T(8,128)}, u32[]{:S(2)}) copy-start(f32[2,128,64,128]{3,2,1,0:T(8,128)} %copy-done) | copy-start | bytes 25165828
  98.7 1.5 copy-start.4
  98.7 1.5 copy-start.5
  100.2 2.2 %copy-start.8 = (f32[65,64]{1,0:T(8,128)S(1)}, f32[65,64]{1,0:T(8,128)}, u32[]{:S(2)}) copy-start(f32[65,64]{1,0:T(8,128)} %get-tuple-element.27) | copy-start | bytes 49924
  100.2 2.2 %copy-start.9 = (f32[65,64]{1,0:T(8,128)S(1)}, f32[65,64]{1,0:T(8,128)}, u32[]{:S(2)}) copy-start(f32[65,64]{1,0:T(8,128)} %get-tuple-element.28) | copy-start | bytes 49924
  110.6 2.0 %copy-start.2 = (f32[128,8192]{1,0:T(8,128)}, f32[128,8192]{1,0:T(8,128)S(1)}, u32[]{:S(2)}) copy-start(f32[128,8192]{1,0:T(8,128)S(1)} %fusion.23) | copy-start | bytes 12582916
  113.6 4.8 %slice-start = ((f32[128,8192]{1,0:T(8,128)}), f32[64,8192]{1,0:T(8,128)S(1)}, s32[]{:S(2)}) async-start(f32[128,8192]{1,0:T(8,128)} %copy-done.2), calls=%async_computation.3 | async-start | bytes 4194304 | tf_op jit(solution)/shard_map/slice | solution.py:103
  116.1 16.6 %copy-start.10 = (f32[128]{0:T(128)S(1)}, f32[128]{0:T(128)}, u32[]{:S(2)}) copy-start(f32[128]{0:T(128)} %param.9) | copy-start | bytes 1540
  116.1 16.6 %collective-permute-start = (bf16[4096,128]{1,0:T(8,128)(2,1)}, bf16[4096,128]{1,0:T(8,128)(2,1)}, u32[]{:S(2)}, u32[]{:S(2)}) collective-permute-start(bf16[4096,128]{1,0:T(8,128)(2,1)} %convert_element_type.128), channel_id=1, source_target_pairs={{0,32},{32,64},{64,96},{96,128},{128,160},{160,192},{192,224},{224... | collective-permute-start | bytes 3145736 | tf_op jit(solution)/shard_map/ppermute | solution.py:13
  119.9 26.6 %copy-start.3 = (bf16[128,4096]{1,0:T(8,128)(2,1)S(1)}, bf16[128,4096]{1,0:T(8,128)(2,1)}, u32[]{:S(2)}) copy-start(bf16[128,4096]{1,0:T(8,128)(2,1)} %param.5) | copy-start | bytes 3145732
  135.9 39.0 %all-to-all-start.1 = ((bf16[32,128,128]{2,1,0:T(8,128)(2,1)}), bf16[32,128,128]{2,1,0:T(8,128)(2,1)S(1)}, u32[]{:S(2)}, u32[]{:S(2)}) async-start(bf16[32,128,128]{2,1,0:T(8,128)(2,1)} %bitcast.25), calls=%async_computation.1 | async-start | bytes 2097152 | tf_op jit(solution)/shard_map/all_to_all | solution.py:110
Sparse Core Ops, SparseCore 0:
  27.8 40.3 all-gather.1
where the time goes:
time: 185 us; the launch traced here: 184 us
  waiting for transfers between devices  80.2 us (43%)
  local copies, waits for them, and re-layouts  35.4 us (19%)
  starting transfers between devices  26.3 us (14%)
  other arithmetic  16.2 us (9%)
  between operations  13.8 us (7%)
  matrix products  12 us (6%)
    all_gather x1, waiting for transfers between devices, local(): all_taps = lax.all_gather(filter_taps, 'seq', axis=0, tiled=True)  39.1 us
    all_to_all x1, waiting for transfers between devices, local(): lax.all_to_all(filtered, 'wide', split_axis=0, concat_axis=1, tiled=True)  27.7 us
    unnamed x30, local copies, waits for them, and re-layouts  15.6 us
    all_to_all x1, starting transfers between devices, local(): lax.all_to_all(gated_values, 'wide', split_axis=1, concat_axis=0, tiled=T...  13.5 us
    ppermute x1, waiting for transfers between devices, passed_along(): return lax.ppermute(value, axis, pairs)  12.7 us
    all_to_all x1, starting transfers between devices, local(): lax.all_to_all(filtered, 'wide', split_axis=0, concat_axis=1, tiled=True)  10.6 us
    rev x1, local copies, waits for them, and re-layouts, causal_filter(): mirrored = jnp.flip(spectrum[:, row_count // 2:], axis=(1, 2))  6.63 us
    dot_general x1, matrix products, causal_filter(): jnp.einsum('panc,pnqk->qakc', turned, column_block(column_count, 1.0), pr...  4.32 us
  transfers between devices with their start and end apart: 4, of which 3 were waited for; matrix products, arithmetic and copies ran while one was open for 4% of the time, Pallas kernels for 0%

commit v1 on v0

--- a/solution.py
+++ b/solution.py
@@ -5,6 +5,28 @@
 from jax.sharding import PartitionSpec as P
 
 PRECISE = lax.Precision.HIGH
+
+
+def in_order(pieces, dim):
+    pieces = jnp.moveaxis(pieces, 0, dim)
+    lengths = pieces.shape
+    return pieces.reshape(*lengths[:dim], lengths[dim] * lengths[dim + 1], *lengths[dim + 2 :])
+
+
+def ring_gather(shard, axis, dim):
+    size = lax.axis_size(axis)
+    pairs = [(i, (i + 1) % size) for i in range(size)]
+    back = [(b, a) for a, b in pairs]
+    lower, upper = ([], [])
+    for step in range(size - 1):
+        if step % 2 == 0:
+            lower.append(lax.ppermute(lower[-1] if lower else shard, axis, pairs))
+        else:
+            upper.append(lax.ppermute(upper[-1] if upper else shard, axis, back))
+    blocks = jnp.stack([*lower[::-1], shard, *upper])
+    shift = lax.axis_index(axis) - len(lower)
+    blocks = blocks[(jnp.arange(size) - shift) % size]
+    return in_order(blocks, dim)
 
 
 def passed_along(value, axis, by):
@@ -95,7 +117,7 @@
 
 def local(out_gate, in_gate, values, filter_taps, skip_gain):
     gated_values = (in_gate.astype(jnp.float32) * values.astype(jnp.float32)).astype(jnp.bfloat16)
-    all_taps = lax.all_gather(filter_taps, "seq", axis=0, tiled=True)
+    all_taps = ring_gather(filter_taps, "seq", 0)
     by_channel = lax.all_to_all(gated_values, "wide", split_axis=1, concat_axis=0, tiled=True)
     group_length = by_channel.shape[0]
     tap_count = all_taps.shape[0]

time: 185 us -> 166 us (0.90)
  the two profiles are of different devices: /device:TPU:18 before, /device:TPU:27 now
where the time goes in v1:
time: 166 us; the launch traced here: 165 us
  starting transfers between devices  53.9 us (32%)
  waiting for transfers between devices  44.5 us (27%)
  local copies, waits for them, and re-layouts  37.9 us (23%)
  other arithmetic  16.7 us (10%)
  matrix products  11.9 us (7%)
    ppermute x8, starting transfers between devices, ring_gather(): lower.append(lax.ppermute(lower[-1] if lower else shard, axis, pairs))  28 us
    all_to_all x1, waiting for transfers between devices, local(): lax.all_to_all(filtered, 'wide', split_axis=0, concat_axis=1, tiled=True)  25.8 us
    unnamed x47, local copies, waits for them, and re-layouts  18.3 us
    all_to_all x1, starting transfers between devices, local(): lax.all_to_all(gated_values, 'wide', split_axis=1, concat_axis=0, tiled=T...  12.9 us
    ppermute x1, waiting for transfers between devices, passed_along(): return lax.ppermute(value, axis, pairs)  10.5 us
    all_to_all x1, starting transfers between devices, local(): lax.all_to_all(filtered, 'wide', split_axis=0, concat_axis=1, tiled=True)  9.21 us
    rev x1, local copies, waits for them, and re-layouts, causal_filter(): mirrored = jnp.flip(spectrum[:, row_count // 2:], axis=(1, 2))  6.62 us
    ppermute x7, waiting for transfers between devices, ring_gather(): upper.append(lax.ppermute(upper[-1] if upper else shard, axis, back))  5.09 us
  transfers between devices with their start and end apart: 18, of which 15 were waited for; matrix products, arithmetic and copies ran while one was open for 9% of the time, Pallas kernels for 0%

profile of v1, /device:TPU:27, one launch (start us, length us, event | category | flops | bytes accessed | tf_op | source)
XLA Modules:
  0.0 165.4 jit_solution(18382404725582557566)
XLA Ops:
  0.0 3.1 %collective-permute-start = (bf16[256,128]{1,0:T(8,128)(2,1)}, bf16[256,128]{1,0:T(8,128)(2,1)S(1)}, u32[]{:S(2)}, u32[]{:S(2)}) collective-permute-start(bf16[256,128]{1,0:T(8,128)(2,1)} %param.8), channel_id=1, source_target_pairs={{0,32},{32,64},{64,96},{96,128},{128,160},{160,192},{192,224},{224... | collective-permute-start | bytes 196616 | tf_op jit(solution)/shard_map/ppermute | solution.py:23
  7.9 12.9 %all-to-all-start = ((bf16[128,32,128]{2,0,1:T(8,128)(2,1)}), bf16[128,32,128]{2,0,1:T(8,128)(2,1)S(1)}, u32[]{:S(2)}, u32[]{:S(2)}) async-start(bf16[128,32,128]{2,0,1:T(8,128)(2,1)} %copy.27), calls=%async_computation | async-start | bytes 2097152 | tf_op jit(solution)/shard_map/all_to_all | solution.py:121
  21.4 3.5 %collective-permute-start.1 = (bf16[256,128]{1,0:T(8,128)(2,1)S(1)}, bf16[256,128]{1,0:T(8,128)(2,1)S(1)}, u32[]{:S(2)}, u32[]{:S(2)}) collective-permute-start(bf16[256,128]{1,0:T(8,128)(2,1)S(1)} %collective-permute-done), channel_id=1, source_target_pairs={{0,32},{32,64},{64,96},{96,128},{128,160},{160,192},{192,224},{224... | collective-permute-start | bytes 196616 | tf_op jit(solution)/shard_map/ppermute | solution.py:23
  26.3 3.6 %collective-permute-start.2 = (bf16[256,128]{1,0:T(8,128)(2,1)S(1)}, bf16[256,128]{1,0:T(8,128)(2,1)S(1)}, u32[]{:S(2)}, u32[]{:S(2)}) collective-permute-start(bf16[256,128]{1,0:T(8,128)(2,1)S(1)} %collective-permute-done.1), channel_id=1, source_target_pairs={{0,32},{32,64},{64,96},{96,128},{128,160},{160,192},{192,224},{224... | collective-permute-start | bytes 196616 | tf_op jit(solution)/shard_map/ppermute | solution.py:23
  31.2 3.6 %collective-permute-start.3 = (bf16[256,128]{1,0:T(8,128)(2,1)S(1)}, bf16[256,128]{1,0:T(8,128)(2,1)S(1)}, u32[]{:S(2)}, u32[]{:S(2)}) collective-permute-start(bf16[256,128]{1,0:T(8,128)(2,1)S(1)} %collective-permute-done.2), channel_id=1, source_target_pairs={{0,32},{32,64},{64,96},{96,128},{128,160},{160,192},{192,224},{224... | collective-permute-start | bytes 196616 | tf_op jit(solution)/shard_map/ppermute | solution.py:23
  36.1 3.6 %collective-permute-start.4 = (bf16[256,128]{1,0:T(8,128)(2,1)S(1)}, bf16[256,128]{1,0:T(8,128)(2,1)S(1)}, u32[]{:S(2)}, u32[]{:S(2)}) collective-permute-start(bf16[256,128]{1,0:T(8,128)(2,1)S(1)} %collective-permute-done.3), channel_id=1, source_target_pairs={{0,32},{32,64},{64,96},{96,128},{128,160},{160,192},{192,224},{224... | collective-permute-start | bytes 196616 | tf_op jit(solution)/shard_map/ppermute | solution.py:23
  41.0 3.6 %collective-permute-start.5 = (bf16[256,128]{1,0:T(8,128)(2,1)S(1)}, bf16[256,128]{1,0:T(8,128)(2,1)S(1)}, u32[]{:S(2)}, u32[]{:S(2)}) collective-permute-start(bf16[256,128]{1,0:T(8,128)(2,1)S(1)} %collective-permute-done.4), channel_id=1, source_target_pairs={{0,32},{32,64},{64,96},{96,128},{128,160},{160,192},{192,224},{224... | collective-permute-start | bytes 196616 | tf_op jit(solution)/shard_map/ppermute | solution.py:23
  45.9 3.6 %collective-permute-start.6 = (bf16[256,128]{1,0:T(8,128)(2,1)S(1)}, bf16[256,128]{1,0:T(8,128)(2,1)S(1)}, u32[]{:S(2)}, u32[]{:S(2)}) collective-permute-start(bf16[256,128]{1,0:T(8,128)(2,1)S(1)} %collective-permute-done.5), channel_id=1, source_target_pairs={{0,32},{32,64},{64,96},{96,128},{128,160},{160,192},{192,224},{224... | collective-permute-start | bytes 196616 | tf_op jit(solution)/shard_map/ppermute | solution.py:23
  50.8 3.6 %collective-permute-start.7 = (bf16[256,128]{1,0:T(8,128)(2,1)S(1)}, bf16[256,128]{1,0:T(8,128)(2,1)S(1)}, u32[]{:S(2)}, u32[]{:S(2)}) collective-permute-start(bf16[256,128]{1,0:T(8,128)(2,1)S(1)} %collective-permute-done.6), channel_id=1, source_target_pairs={{0,32},{32,64},{64,96},{96,128},{128,160},{160,192},{192,224},{224... | collective-permute-start | bytes 196616 | tf_op jit(solution)/shard_map/ppermute | solution.py:23
  62.2 3.3 %fusion.16 = f32[256,8192]{1,0:T(8,128)S(1)} fusion(bf16[64,8192]{1,0:T(8,128)(2,1)S(1)} %reshape_reshape.3, bf16[64,8192]{1,0:T(8,128)(2,1)S(1)} %reshape.278, f32[128,64]{1,0:T(8,128)S(1)} %get-tuple-element.22, f32[128,64]{1,0:T(8,128)S(1)} %get-tuple-element.21, f32[128,64]{1,0:T(8,128)} %fusion.74), kind=kOutput, calls=%fused_computation.32 | convolution fusion | flops 1614905344 | bytes 10584064 | tf_op jit(solution)/shard_map/dot_general | solution.py:82
  67.9 2.6 %fusion.8 = (f32[1,128,64,128]{3,2,0,1:T(8,128)S(1)}, f32[1,128,64,128]{3,2,0,1:T(8,128)S(1)}) fusion(f32[128,64]{1,0:T(8,128)S(1)} %get-tuple-element.23, f32[128,64]{1,0:T(8,128)S(1)} %get-tuple-element.24, f32[1,128,64,128]{3,2,1,0:T(8,128)S(1)} %bitcast.144, f32[1,128,64,128]{3,2,1,0:T(8,128)S(1)} %bitcast.145), kind=kLoop, calls=%fused_computation.14 | loop fusion | flops 6291456 | bytes 16842752 | tf_op jit(solution)/shard_map/sub | solution.py:56
  70.6 4.3 %fusion.12 = f32[2,128,64,128]{3,2,1,0:T(8,128)S(1)} fusion(f32[1,128,64,128]{3,2,0,1:T(8,128)S(1)} %get-tuple-element.8, f32[1,128,64,128]{3,2,0,1:T(8,128)S(1)} %get-tuple-element.7, f32[1,64,2,64]{1,3,0,2:T(8,128)S(1)} %copy-done.6, f32[1,64,2,64]{1,3,0,2:T(8,128)S(1)} %copy-done.7), kind=kOutput, calls=%fused_computation.21 | convolution fusion | flops 1612726272 | bytes 16842752 | tf_op jit(solution)/shard_map/panc,pnqk->qakc/dot_general | solution.py:86
  74.9 2.8 %slice.88 = f32[2,64,64,128]{3,2,1,0:T(8,128)} slice(f32[2,128,64,128]{3,2,1,0:T(8,128)S(1)} %fusion.12), slice={[0:2], [64:128], [0:64], [0:128]} | slice | bytes 8388608 | tf_op jit(solution)/shard_map/slice | solution.py:91
  79.4 6.6 %rev.6 = f32[2,64,64,128]{3,2,1,0:T(8,128)} reverse(f32[2,64,64,128]{3,2,1,0:T(8,128)} %slice.88), dimensions={1,2} | reverse | bytes 8388608 | tf_op jit(solution)/shard_map/jit(_flip)/rev | solution.py:91
  86.1 2.9 %pad_maximum_fusion = f32[2,65,64,128]{3,2,1,0:T(8,128)S(1)} fusion(f32[2,64,64,128]{3,2,1,0:T(8,128)} %rev.6, f32[2,1,63,128]{3,2,1,0:T(8,128)S(1)} %slice.71, f32[2,1,1,128]{3,2,1,0:T(1,128)S(1)} %slice.86), kind=kLoop, calls=%fused_computation.5 | loop fusion | flops 2129920 | bytes 8519680 | tf_op jit(solution)/shard_map/concatenate | solution.py:92
  92.3 2.2 %fusion.13 = f32[2,65,64,128]{3,2,1,0:T(8,128)S(1)} fusion(f32[1,65,64,128]{3,2,1,0:T(8,128)S(1)} %get-tuple-element.6, f32[1,65,64,128]{3,2,1,0:T(8,128)S(1)} %get-tuple-element.5, f32[1,64,2,64]{1,3,2,0:T(8,128)S(1)} %copy-done.5, f32[1,64,2,64]{1,3,2,0:T(8,128)S(1)} %copy-done.4), kind=kOutput, calls=%fused_computation.22 | convolution fusion | flops 818970624 | bytes 8585216 | tf_op jit(solution)/shard_map/pakc,pkqn->qanc/dot_general | solution.py:100
  97.1 3.6 %copy.44 = f32[17,8,64,128]{3,1,2,0:T(8,128)S(1)} copy(f32[17,8,64,128]{3,2,1,0:T(8,128)S(1)} %bitcast.142) | data formatting | bytes 8912896
  100.7 2.1 %fusion.23 = f32[128,8192]{1,0:T(8,128)S(1)} fusion(f32[130,8192]{1,0:T(8,128)S(1)} %bitcast.141, f32[128,65]{1,0:T(8,128)S(1)} %get-tuple-element.20, f32[128,65]{1,0:T(8,128)S(1)} %get-tuple-element.19), kind=kOutput, calls=%fused_computation.43 | convolution fusion | flops 817922560 | bytes 8520704 | tf_op jit(solution)/shard_map/dot_general | solution.py:114
  105.9 2.5 %convert_element_type.128 = bf16[4096,128]{1,0:T(8,128)(2,1)} reshape(bf16[64,8192]{1,0:T(8,128)(2,1)} %slice.143) | data formatting | bytes 2097152 | tf_op jit(solution)/shard_map/convert_element_type | solution.py:127
  108.4 3.7 %collective-permute-start.15 = (bf16[4096,128]{1,0:T(8,128)(2,1)}, bf16[4096,128]{1,0:T(8,128)(2,1)}, u32[]{:S(2)}, u32[]{:S(2)}) collective-permute-start(bf16[4096,128]{1,0:T(8,128)(2,1)} %convert_element_type.128), channel_id=1, source_target_pairs={{0,32},{32,64},{64,96},{96,128},{128,160},{160,192},{192,224},{224... | collective-permute-start | bytes 3145736 | tf_op jit(solution)/shard_map/ppermute | solution.py:35
  113.7 10.5 %collective-permute-done.15 = bf16[4096,128]{1,0:T(8,128)(2,1)} collective-permute-done((bf16[4096,128]{1,0:T(8,128)(2,1)}, bf16[4096,128]{1,0:T(8,128)(2,1)}, u32[]{:S(2)}, u32[]{:S(2)}) %collective-permute-start.15) | collective-permute-done | bytes 1048608 | tf_op jit(solution)/shard_map/ppermute | solution.py:35
  124.2 3.2 %fusion.22 = bf16[4096,128]{1,0:T(8,128)(2,1)} fusion(f32[4096,128]{1,0:T(8,128)} %slice.79, bf16[4096,128]{1,0:T(8,128)(2,1)} %collective-permute-done.15, bf16[128,32,128]{2,0,1:T(8,128)(2,1)S(1)} %all-to-all-done, f32[128]{0:T(128)S(1)} %copy-done.11), kind=kLoop, calls=%fused_computation.40 | loop fusion | flops 3145728 | bytes 5243392 | tf_op jit(solution)/shard_map/convert_element_type | solution.py:129
  127.4 9.2 %all-to-all-start.1 = ((bf16[32,128,128]{2,1,0:T(8,128)(2,1)}), bf16[32,128,128]{2,1,0:T(8,128)(2,1)S(1)}, u32[]{:S(2)}, u32[]{:S(2)}) async-start(bf16[32,128,128]{2,1,0:T(8,128)(2,1)} %bitcast.42), calls=%async_computation.1 | async-start | bytes 2097152 | tf_op jit(solution)/shard_map/all_to_all | solution.py:132
  137.3 25.8 %all-to-all-done.1 = bf16[32,128,128]{2,1,0:T(8,128)(2,1)S(1)} async-done(((bf16[32,128,128]{2,1,0:T(8,128)(2,1)}), bf16[32,128,128]{2,1,0:T(8,128)(2,1)S(1)}, u32[]{:S(2)}, u32[]{:S(2)}) %all-to-all-start.1) | async-done | bytes 1048608 | tf_op jit(solution)/shard_map/all_to_all | solution.py:132
  (99 shorter events, 38.5 us)
Async XLA Ops:
  0.0 21.4 %collective-permute-start = (bf16[256,128]{1,0:T(8,128)(2,1)}, bf16[256,128]{1,0:T(8,128)(2,1)S(1)}, u32[]{:S(2)}, u32[]{:S(2)}) collective-permute-start(bf16[256,128]{1,0:T(8,128)(2,1)} %param.8), channel_id=1, source_target_pairs={{0,32},{32,64},{64,96},{96,128},{128,160},{160,192},{192,224},{224... | collective-permute-start | bytes 196616 | tf_op jit(solution)/shard_map/ppermute | solution.py:23
  3.1 27.1 %collective-permute-start.8 = (bf16[256,128]{1,0:T(8,128)(2,1)}, bf16[256,128]{1,0:T(8,128)(2,1)}, u32[]{:S(2)}, u32[]{:S(2)}) collective-permute-start(bf16[256,128]{1,0:T(8,128)(2,1)} %param.8), channel_id=1, source_target_pairs={{32,0},{64,32},{96,64},{128,96},{160,128},{192,160},{224,192},{256... | collective-permute-start | bytes 196616 | tf_op jit(solution)/shard_map/ppermute | solution.py:25
  7.9 53.7 %all-to-all-start = ((bf16[128,32,128]{2,0,1:T(8,128)(2,1)}), bf16[128,32,128]{2,0,1:T(8,128)(2,1)S(1)}, u32[]{:S(2)}, u32[]{:S(2)}) async-start(bf16[128,32,128]{2,0,1:T(8,128)(2,1)} %copy.27), calls=%async_computation | async-start | bytes 2097152 | tf_op jit(solution)/shard_map/all_to_all | solution.py:121
  21.4 9.8 %copy-start.10 = (bf16[256,128]{1,0:T(8,128)(2,1)}, bf16[256,128]{1,0:T(8,128)(2,1)S(1)}, u32[]{:S(2)}) copy-start(bf16[256,128]{1,0:T(8,128)(2,1)S(1)} %collective-permute-done) | copy-start | bytes 196612
  21.4 4.9 %collective-permute-start.1 = (bf16[256,128]{1,0:T(8,128)(2,1)S(1)}, bf16[256,128]{1,0:T(8,128)(2,1)S(1)}, u32[]{:S(2)}, u32[]{:S(2)}) collective-permute-start(bf16[256,128]{1,0:T(8,128)(2,1)S(1)} %collective-permute-done), channel_id=1, source_target_pairs={{0,32},{32,64},{64,96},{96,128},{128,160},{160,192},{192,224},{224... | collective-permute-start | bytes 196616 | tf_op jit(solution)/shard_map/ppermute | solution.py:23
  26.3 4.9 %collective-permute-start.2 = (bf16[256,128]{1,0:T(8,128)(2,1)S(1)}, bf16[256,128]{1,0:T(8,128)(2,1)S(1)}, u32[]{:S(2)}, u32[]{:S(2)}) collective-permute-start(bf16[256,128]{1,0:T(8,128)(2,1)S(1)} %collective-permute-done.1), channel_id=1, source_target_pairs={{0,32},{32,64},{64,96},{96,128},{128,160},{160,192},{192,224},{224... | collective-permute-start | bytes 196616 | tf_op jit(solution)/shard_map/ppermute | solution.py:23
  30.2 5.4 %collective-permute-start.9 = (bf16[256,128]{1,0:T(8,128)(2,1)}, bf16[256,128]{1,0:T(8,128)(2,1)S(1)}, u32[]{:S(2)}, u32[]{:S(2)}) collective-permute-start(bf16[256,128]{1,0:T(8,128)(2,1)} %collective-permute-done.8), channel_id=1, source_target_pairs={{32,0},{64,32},{96,64},{128,96},{160,128},{192,160},{224,192},{256... | collective-permute-start | bytes 196616 | tf_op jit(solution)/shard_map/ppermute | solution.py:25
  31.2 4.9 %collective-permute-start.3 = (bf16[256,128]{1,0:T(8,128)(2,1)S(1)}, bf16[256,128]{1,0:T(8,128)(2,1)S(1)}, u32[]{:S(2)}, u32[]{:S(2)}) collective-permute-start(bf16[256,128]{1,0:T(8,128)(2,1)S(1)} %collective-permute-done.2), channel_id=1, source_target_pairs={{0,32},{32,64},{64,96},{96,128},{128,160},{160,192},{192,224},{224... | collective-permute-start | bytes 196616 | tf_op jit(solution)/shard_map/ppermute | solution.py:23
  35.6 5.2 %collective-permute-start.10 = (bf16[256,128]{1,0:T(8,128)(2,1)S(1)}, bf16[256,128]{1,0:T(8,128)(2,1)S(1)}, u32[]{:S(2)}, u32[]{:S(2)}) collective-permute-start(bf16[256,128]{1,0:T(8,128)(2,1)S(1)} %collective-permute-done.9), channel_id=1, source_target_pairs={{32,0},{64,32},{96,64},{128,96},{160,128},{192,160},{224,192},{256... | collective-permute-start | bytes 196616 | tf_op jit(solution)/shard_map/ppermute | solution.py:25
  36.1 4.9 %collective-permute-start.4 = (bf16[256,128]{1,0:T(8,128)(2,1)S(1)}, bf16[256,128]{1,0:T(8,128)(2,1)S(1)}, u32[]{:S(2)}, u32[]{:S(2)}) collective-permute-start(bf16[256,128]{1,0:T(8,128)(2,1)S(1)} %collective-permute-done.3), channel_id=1, source_target_pairs={{0,32},{32,64},{64,96},{96,128},{128,160},{160,192},{192,224},{224... | collective-permute-start | bytes 196616 | tf_op jit(solution)/shard_map/ppermute | solution.py:23
  40.8 4.9 %collective-permute-start.11 = (bf16[256,128]{1,0:T(8,128)(2,1)S(1)}, bf16[256,128]{1,0:T(8,128)(2,1)S(1)}, u32[]{:S(2)}, u32[]{:S(2)}) collective-permute-start(bf16[256,128]{1,0:T(8,128)(2,1)S(1)} %collective-permute-done.10), channel_id=1, source_target_pairs={{32,0},{64,32},{96,64},{128,96},{160,128},{192,160},{224,192},{256... | collective-permute-start | bytes 196616 | tf_op jit(solution)/shard_map/ppermute | solution.py:25
  41.0 4.9 %collective-permute-start.5 = (bf16[256,128]{1,0:T(8,128)(2,1)S(1)}, bf16[256,128]{1,0:T(8,128)(2,1)S(1)}, u32[]{:S(2)}, u32[]{:S(2)}) collective-permute-start(bf16[256,128]{1,0:T(8,128)(2,1)S(1)} %collective-permute-done.4), channel_id=1, source_target_pairs={{0,32},{32,64},{64,96},{96,128},{128,160},{160,192},{192,224},{224... | collective-permute-start | bytes 196616 | tf_op jit(solution)/shard_map/ppermute | solution.py:23
  45.7 4.9 %collective-permute-start.12 = (bf16[256,128]{1,0:T(8,128)(2,1)S(1)}, bf16[256,128]{1,0:T(8,128)(2,1)S(1)}, u32[]{:S(2)}, u32[]{:S(2)}) collective-permute-start(bf16[256,128]{1,0:T(8,128)(2,1)S(1)} %collective-permute-done.11), channel_id=1, source_target_pairs={{32,0},{64,32},{96,64},{128,96},{160,128},{192,160},{224,192},{256... | collective-permute-start | bytes 196616 | tf_op jit(solution)/shard_map/ppermute | solution.py:25
  45.9 4.9 %collective-permute-start.6 = (bf16[256,128]{1,0:T(8,128)(2,1)S(1)}, bf16[256,128]{1,0:T(8,128)(2,1)S(1)}, u32[]{:S(2)}, u32[]{:S(2)}) collective-permute-start(bf16[256,128]{1,0:T(8,128)(2,1)S(1)} %collective-permute-done.5), channel_id=1, source_target_pairs={{0,32},{32,64},{64,96},{96,128},{128,160},{160,192},{192,224},{224... | collective-permute-start | bytes 196616 | tf_op jit(solution)/shard_map/ppermute | solution.py:23
  50.6 4.9 %collective-permute-start.13 = (bf16[256,128]{1,0:T(8,128)(2,1)S(1)}, bf16[256,128]{1,0:T(8,128)(2,1)S(1)}, u32[]{:S(2)}, u32[]{:S(2)}) collective-permute-start(bf16[256,128]{1,0:T(8,128)(2,1)S(1)} %collective-permute-done.12), channel_id=1, source_target_pairs={{32,0},{64,32},{96,64},{128,96},{160,128},{192,160},{224,192},{256... | collective-permute-start | bytes 196616 | tf_op jit(solution)/shard_map/ppermute | solution.py:25
  50.8 4.9 %collective-permute-start.7 = (bf16[256,128]{1,0:T(8,128)(2,1)S(1)}, bf16[256,128]{1,0:T(8,128)(2,1)S(1)}, u32[]{:S(2)}, u32[]{:S(2)}) collective-permute-start(bf16[256,128]{1,0:T(8,128)(2,1)S(1)} %collective-permute-done.6), channel_id=1, source_target_pairs={{0,32},{32,64},{64,96},{96,128},{128,160},{160,192},{192,224},{224... | collective-permute-start | bytes 196616 | tf_op jit(solution)/shard_map/ppermute | solution.py:23
  55.5 4.9 %collective-permute-start.14 = (bf16[256,128]{1,0:T(8,128)(2,1)S(1)}, bf16[256,128]{1,0:T(8,128)(2,1)S(1)}, u32[]{:S(2)}, u32[]{:S(2)}) collective-permute-start(bf16[256,128]{1,0:T(8,128)(2,1)S(1)} %collective-permute-done.13), channel_id=1, source_target_pairs={{32,0},{64,32},{96,64},{128,96},{160,128},{192,160},{224,192},{256... | collective-permute-start | bytes 196616 | tf_op jit(solution)/shard_map/ppermute | solution.py:25
  74.9 4.5 %copy-start = (f32[2,128,64,128]{3,2,1,0:T(8,128)}, f32[2,128,64,128]{3,2,1,0:T(8,128)S(1)}, u32[]{:S(2)}) copy-start(f32[2,128,64,128]{3,2,1,0:T(8,128)S(1)} %fusion.12) | copy-start | bytes 25165828
  86.1 4.6 %copy-start.1 = (f32[2,128,64,128]{3,2,1,0:T(8,128)S(1)}, f32[2,128,64,128]{3,2,1,0:T(8,128)}, u32[]{:S(2)}) copy-start(f32[2,128,64,128]{3,2,1,0:T(8,128)} %copy-done) | copy-start | bytes 25165828
  105.9 6.2 %slice-start = ((f32[128,8192]{1,0:T(8,128)}), f32[64,8192]{1,0:T(8,128)S(1)}, s32[]{:S(2)}) async-start(f32[128,8192]{1,0:T(8,128)} %copy-done.2), calls=%async_computation.2 | async-start | bytes 4194304 | tf_op jit(solution)/shard_map/slice | solution.py:125
  108.4 15.8 %copy-start.11 = (f32[128]{0:T(128)S(1)}, f32[128]{0:T(128)}, u32[]{:S(2)}) copy-start(f32[128]{0:T(128)} %param.9) | copy-start | bytes 1540
  108.4 15.8 %collective-permute-start.15 = (bf16[4096,128]{1,0:T(8,128)(2,1)}, bf16[4096,128]{1,0:T(8,128)(2,1)}, u32[]{:S(2)}, u32[]{:S(2)}) collective-permute-start(bf16[4096,128]{1,0:T(8,128)(2,1)} %convert_element_type.128), channel_id=1, source_target_pairs={{0,32},{32,64},{64,96},{96,128},{128,160},{160,192},{192,224},{224... | collective-permute-start | bytes 3145736 | tf_op jit(solution)/shard_map/ppermute | solution.py:35
  113.7 22.9 %copy-start.3 = (bf16[128,4096]{1,0:T(8,128)(2,1)S(1)}, bf16[128,4096]{1,0:T(8,128)(2,1)}, u32[]{:S(2)}) copy-start(bf16[128,4096]{1,0:T(8,128)(2,1)} %param.5) | copy-start | bytes 3145732
  127.4 35.7 %all-to-all-start.1 = ((bf16[32,128,128]{2,1,0:T(8,128)(2,1)}), bf16[32,128,128]{2,1,0:T(8,128)(2,1)S(1)}, u32[]{:S(2)}, u32[]{:S(2)}) async-start(bf16[32,128,128]{2,1,0:T(8,128)(2,1)} %bitcast.42), calls=%async_computation.1 | async-start | bytes 2097152 | tf_op jit(solution)/shard_map/all_to_all | solution.py:132
  (7 other events, 14.9 us)
